TPU v7x, 128 devices: a whole 4x4x4 slice. The times are simulated.
128 devices in a mesh: dp: 8 (over x, core), fsdp: 16 (over y, z).
Axes of the slice: x: 4, y: 4, z: 4, core: 2. Of those that a mesh axis runs over, the one named last changes fastest.
Arguments:
- tokens: bfloat16 [256, 256, 768], P(('dp', 'fsdp')), may hold values from -24 to 24
- lengths: int32 [256], P(('dp', 'fsdp')), may hold values from 128 to 256, as said below
- positions: int32 [256, 64], P(('dp', 'fsdp')), may hold values from 0 to 127
- cotangent: bfloat16 [256, 64, 768], P(('dp', 'fsdp')), may hold values from -24 to 24
- qkv_weight: bfloat16 [768, 2304], P(('dp', 'fsdp')), may hold values from -0.21875 to 0.21875
- out_weight: bfloat16 [768, 768], P(('dp', 'fsdp')), may hold values from -1.25 to 1.25
- up_weight: bfloat16 [768, 3072], P(('dp', 'fsdp')), may hold values from -0.21875 to 0.21875
- down_weight: bfloat16 [3072, 768], P(('dp', 'fsdp')), may hold values from -0.109375 to 0.109375
- norm_gains: bfloat16 [2, 768], P(None, ('dp', 'fsdp')), may hold values from 0.25 to 1.75
- biases: bfloat16 [6, 768], P(None, ('dp', 'fsdp')), may hold values from -3 to 3
- up_bias: bfloat16 [3072], P(('dp', 'fsdp')), may hold values from -3 to 3
Outputs:
- mixed: bfloat16 [256, 256, 768], P(('dp', 'fsdp'))
- token_grad: float32 [256, 256, 768], P(('dp', 'fsdp'))
- qkv_grad: float32 [768, 2304], P(('dp', 'fsdp'))
- out_grad: float32 [768, 768], P(('dp', 'fsdp'))
- up_grad: float32 [768, 3072], P(('dp', 'fsdp'))
- down_grad: float32 [3072, 768], P(('dp', 'fsdp'))
- gains_grad: float32 [2, 768], P(None, ('dp', 'fsdp'))
- biases_grad: float32 [6, 768], P(None, ('dp', 'fsdp'))
- up_bias_grad: float32 [3072], P(('dp', 'fsdp'))
Inputs may be any that keep to these rules, and one draw needn't show every extreme that they name: `lengths`: one cell in every draw has exactly 256 genes; the other slots of a cell are padding. `positions`: all lie below 128, so within the cell's genes; a row may repeat, and repeated rows add.
All inputs are finite; a program needn't handle non-finite values.
Results may differ from a plain program's by a relative error of at most 0.012.
Values may be sent and summed in bfloat16 or wider, within the bound.
No kernel may reach another device: no remote copies, remote signals or barrier semaphores. Data moves between devices by JAX's collectives and lax.ppermute only.
A program may use at most 192 MiB of HBM per device.

v0:
```python
import jax
import jax.numpy as jnp
from jax import lax
from jax.sharding import PartitionSpec as P

HEAD_DIM = 64


def in_one_piece(arrays, axis, dim, along):
    ends, at = ([], 0)
    for a in arrays[:-1]:
        at += a.shape[along]
        ends.append(at)
    both = jnp.concatenate(arrays, axis=along)
    return tuple(jnp.split(lax.all_gather(both, axis, axis=dim, tiled=True), ends, axis=along))


def split_up(shard, dim, count):
    lengths = shard.shape
    tiles = shard.reshape(*lengths[:dim], count, lengths[dim] // count, *lengths[dim + 1 :])
    return jnp.moveaxis(tiles, dim, 0)


def sum_packed(arrays, axis, dims):
    count = lax.axis_size(axis)
    tiles = [split_up(a, dim, count) for a, dim in zip(arrays, dims)]
    lines = jnp.concatenate([b.reshape(count, -1) for b in tiles], axis=1)
    extent = max(16, -(-lines.shape[1] // 1024) * 8)
    lines = jnp.pad(lines, ((0, 0), (0, extent * 128 - lines.shape[1]))).reshape(-1, 128)
    line, at, done = (lax.psum_scatter(lines, axis, tiled=True).reshape(-1), 0, [])
    for b in tiles:
        part = b[0]
        done.append(line[at : at + part.size].reshape(part.shape))
        at += part.size
    return tuple(done)


def layer_norm(inputs, gain, shift):
    center_mean = jnp.mean(inputs, axis=-1, keepdims=True)
    centered = inputs - center_mean
    variance = jnp.mean(centered * centered, axis=-1, keepdims=True)
    return centered * lax.rsqrt(variance + 1e-05) * gain + shift


def gelu_exact(values):
    return jax.nn.gelu(values, approximate=False)


def forward(inputs, valid_keys, weights):
    qkv_weight, out_weight, up_weight, down_weight, norm_gains, biases, up_bias = weights
    num_cells, length, model_width = inputs.shape
    head_count = model_width // HEAD_DIM
    gains_f = norm_gains.astype(jnp.float32)
    biases_f = biases.astype(jnp.float32)
    low_one = layer_norm(inputs, gains_f[0], biases_f[0]).astype(jnp.bfloat16)
    qkv_shift = jnp.concatenate([biases_f[1], jnp.zeros_like(biases_f[1]), biases_f[2]])
    qkv_low = (
        jnp.einsum("cld,de->cle", low_one, qkv_weight, preferred_element_type=jnp.float32)
        + qkv_shift
    ).astype(jnp.bfloat16)
    parts = qkv_low.reshape(num_cells, length, 3, head_count, HEAD_DIM)
    queries = parts[:, :, 0]
    key_rows = parts[:, :, 1]
    value_rows = parts[:, :, 2]
    scores = jnp.einsum(
        "cqhe,ckhe->chqk", queries, key_rows, preferred_element_type=jnp.float32
    ) * HEAD_DIM ** (-0.5)
    scores = jnp.where(valid_keys[:, None, None, :], scores, -1000000000.0)
    row_peak = jnp.max(scores, axis=-1, keepdims=True)
    exp_scores = jnp.exp(scores - row_peak)
    soft_weights = exp_scores / jnp.sum(exp_scores, axis=-1, keepdims=True)
    soft_low = soft_weights.astype(jnp.bfloat16)
    attended = jnp.einsum(
        "chqk,ckhe->cqhe", soft_low, value_rows, preferred_element_type=jnp.float32
    )
    attended = attended.reshape(num_cells, length, model_width).astype(jnp.bfloat16)
    mid_stream = (
        inputs
        + jnp.einsum("cld,de->cle", attended, out_weight, preferred_element_type=jnp.float32)
        + biases_f[3]
    )
    low_two = layer_norm(mid_stream, gains_f[1], biases_f[4]).astype(jnp.bfloat16)
    up_pre = jnp.einsum(
        "cld,df->clf", low_two, up_weight, preferred_element_type=jnp.float32
    ) + up_bias.astype(jnp.float32)
    activated = gelu_exact(up_pre).astype(jnp.bfloat16)
    layer_out = (
        mid_stream
        + jnp.einsum("clf,fd->cld", activated, down_weight, preferred_element_type=jnp.float32)
        + biases_f[5]
    )
    saved = (
        low_one,
        queries,
        key_rows,
        value_rows,
        soft_weights,
        soft_low,
        attended,
        mid_stream,
        low_two,
        up_pre,
        activated,
    )
    return (layer_out, saved)


def backward(inputs, weights, saved, positions, cotangent):
    qkv_weight, out_weight, up_weight, down_weight, norm_gains, biases, up_bias = weights
    (
        low_one,
        queries,
        key_rows,
        value_rows,
        soft_weights,
        soft_low,
        attended,
        mid_stream,
        low_two,
        up_pre,
        activated,
    ) = saved
    num_cells, length, model_width = inputs.shape
    gains_f = norm_gains.astype(jnp.float32)
    biases_f = biases.astype(jnp.float32)
    head_scale = HEAD_DIM ** (-0.5)

    def scatter_rows(where_rows, rows):
        return jnp.zeros((length, model_width), jnp.float32).at[where_rows].add(rows)

    out_cot = jax.vmap(scatter_rows)(positions, cotangent.astype(jnp.float32))
    down_in = out_cot.astype(jnp.bfloat16)
    grad_down = jnp.einsum("clf,cld->fd", activated, down_in, preferred_element_type=jnp.float32)
    grad_down_bias = jnp.sum(down_in.astype(jnp.float32), axis=(0, 1))
    grad_act = jnp.einsum("cld,fd->clf", down_in, down_weight, preferred_element_type=jnp.float32)
    _, gelu_pull = jax.vjp(gelu_exact, up_pre)
    pre_low = gelu_pull(grad_act)[0].astype(jnp.bfloat16)
    grad_up = jnp.einsum("cld,clf->df", low_two, pre_low, preferred_element_type=jnp.float32)
    grad_up_bias = jnp.sum(pre_low.astype(jnp.float32), axis=(0, 1))
    grad_norm_two = jnp.einsum(
        "clf,df->cld", pre_low, up_weight, preferred_element_type=jnp.float32
    )
    _, norm_pull_two = jax.vjp(layer_norm, mid_stream, gains_f[1], biases_f[4])
    grad_mid_norm, grad_gain_two, grad_shift_two = norm_pull_two(grad_norm_two)
    grad_mid = out_cot + grad_mid_norm
    branch_low = grad_mid.astype(jnp.bfloat16)
    grad_out_w = jnp.einsum("cld,cle->de", attended, branch_low, preferred_element_type=jnp.float32)
    grad_out_bias = jnp.sum(branch_low.astype(jnp.float32), axis=(0, 1))
    grad_att = jnp.einsum(
        "cle,de->cld", branch_low, out_weight, preferred_element_type=jnp.float32
    ).astype(jnp.bfloat16)
    grad_att = grad_att.reshape(num_cells, length, model_width // HEAD_DIM, HEAD_DIM)
    grad_soft = jnp.einsum(
        "cqhe,ckhe->chqk", grad_att, value_rows, preferred_element_type=jnp.float32
    )
    grad_values = jnp.einsum(
        "chqk,cqhe->ckhe", soft_low, grad_att, preferred_element_type=jnp.float32
    )
    grad_scores = soft_weights * (
        grad_soft - jnp.sum(grad_soft * soft_weights, axis=-1, keepdims=True)
    )
    scores_low = grad_scores.astype(jnp.bfloat16)
    grad_queries = (
        jnp.einsum("chqk,ckhe->cqhe", scores_low, key_rows, preferred_element_type=jnp.float32)
        * head_scale
    )
    grad_keys = (
        jnp.einsum("chqk,cqhe->ckhe", scores_low, queries, preferred_element_type=jnp.float32)
        * head_scale
    )
    grad_qkv = (
        jnp.stack([grad_queries, grad_keys, grad_values], axis=2)
        .reshape(num_cells, length, 3 * model_width)
        .astype(jnp.bfloat16)
    )
    grad_qkv_w = jnp.einsum("cld,cle->de", low_one, grad_qkv, preferred_element_type=jnp.float32)
    qkv_sums = jnp.sum(grad_qkv.astype(jnp.float32), axis=(0, 1))
    grad_norm_one = jnp.einsum(
        "cle,de->cld", grad_qkv, qkv_weight, preferred_element_type=jnp.float32
    )
    _, norm_pull_one = jax.vjp(layer_norm, inputs, gains_f[0], biases_f[0])
    grad_in_norm, grad_gain_one, grad_shift_one = norm_pull_one(grad_norm_one)
    token_grad = grad_mid + grad_in_norm
    attn_vectors = jnp.stack(
        [
            grad_gain_one,
            grad_shift_one,
            qkv_sums[:model_width],
            qkv_sums[2 * model_width :],
            grad_out_bias,
        ]
    )
    mlp_vectors = jnp.stack([grad_gain_two, grad_shift_two, grad_down_bias])
    return (
        token_grad,
        grad_qkv_w,
        grad_out_w,
        grad_up,
        grad_down,
        grad_up_bias,
        attn_vectors,
        mlp_vectors,
    )


def local(
    tokens,
    lengths,
    positions,
    cotangent,
    qkv_weight,
    out_weight,
    up_weight,
    down_weight,
    norm_gains,
    biases,
    up_bias,
):
    inputs = tokens.astype(jnp.float32)
    row_index = jnp.arange(tokens.shape[1], dtype=jnp.int32)
    valid_keys = row_index[None, :] < lengths[:, None]
    gathered = (
        *in_one_piece((qkv_weight, out_weight, up_weight), ("dp", "fsdp"), 0, 1),
        lax.all_gather(down_weight, ("dp", "fsdp"), axis=0, tiled=True),
        *in_one_piece((norm_gains, biases), ("dp", "fsdp"), 1, 0),
        lax.all_gather(up_bias, ("dp", "fsdp"), axis=0, tiled=True),
    )
    layer_out, saved = forward(inputs, valid_keys, gathered)
    again = (
        *in_one_piece((qkv_weight, out_weight, up_weight), ("dp", "fsdp"), 0, 1),
        lax.all_gather(down_weight, ("dp", "fsdp"), axis=0, tiled=True),
        *in_one_piece((norm_gains, biases), ("dp", "fsdp"), 1, 0),
        lax.all_gather(up_bias, ("dp", "fsdp"), axis=0, tiled=True),
    )
    _, saved_again = forward(inputs, valid_keys, again)
    (
        token_grad,
        grad_qkv_w,
        grad_out_w,
        grad_up,
        grad_down,
        grad_up_bias,
        attn_vectors,
        mlp_vectors,
    ) = backward(inputs, again, saved_again, positions, cotangent)
    gains_all = jnp.stack([attn_vectors[0], mlp_vectors[0]])
    biases_all = jnp.stack(
        [
            attn_vectors[1],
            attn_vectors[2],
            attn_vectors[3],
            attn_vectors[4],
            mlp_vectors[1],
            mlp_vectors[2],
        ]
    )
    qkv_shard, out_shard, up_shard, down_shard, gains_shard, biases_shard, up_bias_shard = (
        sum_packed(
            (grad_qkv_w, grad_out_w, grad_up, grad_down, gains_all, biases_all, grad_up_bias),
            ("dp", "fsdp"),
            (0, 0, 0, 0, 1, 1, 0),
        )
    )
    return (
        layer_out.astype(jnp.bfloat16),
        token_grad,
        qkv_shard,
        out_shard,
        up_shard,
        down_shard,
        gains_shard,
        biases_shard,
        up_bias_shard,
    )


def solution(mesh):
    in_specs = (
        P(("dp", "fsdp"), None, None),
        P(("dp", "fsdp")),
        P(("dp", "fsdp"), None),
        P(("dp", "fsdp"), None, None),
        P(("dp", "fsdp"), None),
        P(("dp", "fsdp"), None),
        P(("dp", "fsdp"), None),
        P(("dp", "fsdp"), None),
        P(None, ("dp", "fsdp")),
        P(None, ("dp", "fsdp")),
        P(("dp", "fsdp")),
    )
    out_specs = (
        P(("dp", "fsdp"), None, None),
        P(("dp", "fsdp"), None, None),
        P(("dp", "fsdp"), None),
        P(("dp", "fsdp"), None),
        P(("dp", "fsdp"), None),
        P(("dp", "fsdp"), None),
        P(None, ("dp", "fsdp")),
        P(None, ("dp", "fsdp")),
        P(("dp", "fsdp")),
    )
    return jax.shard_map(local, mesh=mesh, in_specs=in_specs, out_specs=out_specs, check_vma=False)
```

profile of v0, /device:TPU:32, one launch (start us, length us, event | category | flops | bytes accessed | tf_op | source)
XLA Modules:
  0.0 631.7 jit_solution(10611986929493141157)
XLA Ops:
  11.1 59.9 %all-gather = bf16[128,6,8]{2,1,0:T(8,128)(2,1)S(1)} all-gather(bf16[1,6,8]{2,1,0:T(8,128)(2,1)S(1)} %maximum_bitcast_fusion.2), channel_id=1, replica_groups=mesh['dp'=8,'fsdp'=16] {'dp','fsdp'}, dimensions={0}, use_global_device_ids=true | all-gather | bytes 12384 | tf_op jit(solution)/shard_map/all_gather | solution.py:15
  73.7 65.0 %all-reduce.1 = bf16[3072]{0:T(1024)(128)(2,1)S(1)} all-reduce(bf16[3072]{0:T(1024)(128)(2,1)S(1)} %dynamic-update-slice), channel_id=1, replica_groups=mesh['dp'=8,'fsdp'=16] {'dp','fsdp'}, use_global_device_ids=true, to_apply=%add.1 | all-reduce | flops 3072 | bytes 12288
  141.3 7.9 %scatter_fusion = f32[2,256,768]{2,1,0:T(8,128)S(1)} fusion(f32[2,256,768]{2,1,0:T(8,128)S(1)} %broadcast_in_dim.30, s32[128]{0:T(128)S(1)} %reshape.199, f32[128,768]{1,0:T(8,128)S(1)} %bitcast_convert_fusion), kind=kCustom, calls=%fused_computation | custom fusion | flops 98304 | bytes 1180672 | tf_op jit(solution)/shard_map/vmap()/scatter-add | solution.py:129
  149.6 14.5 %reshape.210 = bf16[768,6144]{1,0:T(8,128)(2,1)} reshape(bf16[128,6,6144]{2,1,0:T(8,128)(2,1)} %all-gather.7.cloned.1.call-done) | data formatting | bytes 18874368
  164.1 5.6 fusion.12
  169.7 4.3 copy.61
  176.4 2.9 fusion.67
  179.3 2.5 fusion.44
  183.5 4.4 fusion.38
  187.9 2.6 copy-done.5
  190.5 15.9 %multiply_convert_fusion.1 = (bf16[2,256,3072]{2,1,0:T(8,128)(2,1)}, f32[2,256,3072]{2,1,0:T(8,128)}) fusion(f32[2,256,3072]{2,1,0:T(8,128)S(1)} %get-tuple-element.44, f32[3072]{0:T(1024)S(1)} %convert_element_type.99, u8[256,3072]{1,0:T(8,128)(4,1)S(1)} %get-tuple-element.10, u8[256,3072]{1,0:T(8,128)(4,1)S(1)} %get-tuple-element.9), kind=kLoop, calls=%fused_computation.13 | loop fusion | flops 111673344 | bytes 17313792 | tf_op jit(solution)/shard_map/convert_element_type | solution.py:86
  206.4 9.0 %convert_reduce_fusion = (f32[3072]{0:T(1024)S(1)}, bf16[2,256,3072]{2,1,0:T(8,128)(2,1)S(1)}) fusion(f32[2,256,3072]{2,1,0:T(8,128)} %get-tuple-element.33, bf16[3072,768]{1,0:T(8,128)(2,1)} %all-gather.5.cloned.1.call-done, f32[2,256,768]{2,1,0:T(8,128)S(1)} %scatter_fusion, f32[2,256,3072]{2,1,0:T(8,128)} %copy-done.5, f32[3072]{0:T(1024)S(1)} %convert_element_type.99), kind=kOutput, calls=%fused_computation.9 | convolution fusion | flops 2443047936 | bytes 22044672 | tf_op jit(solution)/shard_map/cld,fd->clf/dot_general | solution.py:135
  215.5 6.5 %multiply_reduce_fusion.1 = (f32[768]{0:T(1024)S(1)}, f32[2,256]{1,0:T(2,128)S(1)}, f32[768]{0:T(1024)S(1)}, f32[2,256,768]{2,1,0:T(8,128)S(1)}) fusion(f32[2,256,768]{2,1,0:T(8,128)S(1)} %copy-done.7, f32[2,256]{1,0:T(2,128)S(1)} %fusion.55, f32[2,256]{1,0:T(2,128)S(1)} %broadcast_multiply_fusion, f32[768]{0:T(1024)S(1)} %get-tuple-element.52, ...), kind=kOutput, calls=%fused_computation.69 | convolution fusion | flops 2419062784 | bytes 11025408 | tf_op jit(solution)/shard_map/clf,df->cld/dot_general | solution.py:140
  223.7 3.0 convolution_convert_fusion
  229.0 4.2 fusion.39
  233.2 6.8 %multiply_reduce_fusion = (f32[2,12,256]{2,1,0:T(8,128)S(1)}, f32[2,12,256,256]{2,3,1,0:T(8,128)}) fusion(f32[2,12,256,256]{2,3,1,0:T(8,128)} %copy-done.9, f32[2,12,256]{2,1,0:T(8,128)S(1)} %get-tuple-element.40, bf16[2,256,12,64]{1,3,2,0:T(8,128)(2,1)S(1)} %bitcast.130, bf16[2,256,3,12,64]{1,4,3,2,0:T(8,128)(2,1)S(1)} %bitcast.120), kind=kOutput, calls=%fused_computation.11 | convolution fusion | flops 206039040 | bytes 14213120 | tf_op jit(solution)/shard_map/cqhe,ckhe->chqk/dot_general | solution.py:153
  240.1 4.3 multiply_convert_fusion
  247.2 4.3 fusion.62
  251.5 5.4 convolution_bitcast_fusion
  259.1 5.5 convolution_bitcast_fusion.2
  267.2 8.3 %reshape_reshape.12 = f32[128,13824]{1,0:T(8,128)} reshape(f32[768,2304]{1,0:T(8,128)} %convolution_bitcast_fusion) | data formatting | bytes 14155776 | tf_op jit(solution)/shard_map/reshape;reshape | solution.py:27
  275.5 6.5 %constant_dynamic-update-slice_fusion.9 = f32[128,55368]{1,0:T(8,128)} fusion(f32[128,13824]{1,0:T(8,128)} %reshape_reshape.12), kind=kLoop, calls=%fused_computation.107 | loop fusion | bytes 14155776
  281.9 3.0 reshape_reshape.13
  285.0 11.3 %reshape_reshape.14 = f32[128,18432]{1,0:T(8,128)} reshape(f32[768,3072]{1,0:T(8,128)} %convolution_bitcast_fusion.2) | data formatting | bytes 18874368 | tf_op jit(solution)/shard_map/reshape;reshape | solution.py:27
  296.3 8.1 %convolution_bitcast_fusion.1 = f32[3072,768]{1,0:T(8,128)} fusion(bf16[2,256,3072]{2,1,0:T(8,128)(2,1)} %get-tuple-element.32, f32[2,256,768]{2,1,0:T(8,128)S(1)} %scatter_fusion), kind=kOutput, calls=%fused_computation.29 | convolution fusion | flops 2416312320 | bytes 14155776 | tf_op jit(solution)/shard_map/clf,cld->fd/dot_general | solution.py:133
  304.4 10.2 %reshape_reshape.15 = f32[128,18432]{1,0:T(8,128)} reshape(f32[3072,768]{1,0:T(8,128)} %convolution_bitcast_fusion.1) | data formatting | bytes 18874368 | tf_op jit(solution)/shard_map/reshape;reshape | solution.py:27
  318.4 8.8 %constant_dynamic-update-slice_fusion.7 = f32[128,55368]{1,0:T(8,128)} fusion(f32[128,55368]{1,0:T(8,128)} %constant_dynamic-update-slice_fusion.8, f32[128,18432]{1,0:T(8,128)} %reshape_reshape.14), kind=kLoop, calls=%fused_computation.105 | loop fusion | bytes 18874368
  327.1 4.2 constant_dynamic-update-slice_fusion.6
  336.0 20.7 %pad.4 = f32[128,56320]{1,0:T(8,128)} pad(f32[128,55368]{1,0:T(8,128)} %dynamic-update-slice.7, f32[]{:T(128)} %constant.39.clone.1), padding=0_0x0_952 | pad | bytes 57184260 | tf_op jit(solution)/shard_map/jit(_pad)/pad | solution.py:29
  356.7 25.5 %reshape.191 = f32[56320,128]{1,0:T(8,128)} reshape(f32[128,56320]{1,0:T(8,128)} %pad.4) | data formatting | bytes 57671680 | tf_op jit(solution)/shard_map/reshape | solution.py:29
  384.1 6.3 add_convert_fusion.1
  390.4 226.5 %all-reduce.5.cloned.1.call-done = f32[56320,128]{1,0:T(8,128)} async-done(((f32[56320,128]{1,0:T(8,128)}), f32[56320,128]{1,0:T(8,128)}) %all-reduce.5.cloned.1.call-update) | async-done | bytes 28835856
  (153 shorter events, 43.4 us)
Async XLA Ops:
  7.2 142.4 %all-gather.7.cloned.1.call-start = ((), (), s32[]{:S(2)}) async-start(), calls=%async_computation.1 | async-start | bytes 12681216 | tf_op jit(solution)/shard_map/all_gather | solution.py:15
  8.7 197.7 %all-gather.5.cloned.1.call-start = ((), (), s32[]{:S(2)}) async-start(), calls=%async_computation | async-start | bytes 4755456 | tf_op jit(solution)/shard_map/all_gather | solution.py:224
  9.5 607.4 %all-reduce.5.cloned.1.call-start = ((), (), s32[]{:S(2)}) async-start(), calls=%async_computation.2 | async-start | bytes 57671680
  72.7 76.5 %copy-start.2 = (bf16[2,256,768]{2,1,0:T(8,128)(2,1)S(1)}, bf16[2,256,768]{2,1,0:T(8,128)(2,1)}, u32[]{:S(2)}) copy-start(bf16[2,256,768]{2,1,0:T(8,128)(2,1)} %param.11) | copy-start | bytes 2359300
  140.5 9.0 %copy-start.16 = (s32[2]{0:T(128)S(1)}, s32[2]{0:T(128)}, u32[]{:S(2)}) copy-start(s32[2]{0:T(128)} %param.12) | copy-start | bytes 28
  176.4 5.6 slice-start.3
  176.4 5.6 slice-start.4
  179.3 2.8 copy-start.9
  179.3 3.0 slice-start.5
  182.0 1.5 copy-start.13
  183.2 4.8 copy-start.6
  187.9 2.6 copy-start.5
  206.4 9.0 %copy-start.7 = (f32[2,256,768]{2,1,0:T(8,128)S(1)}, f32[2,256,768]{2,1,0:T(8,128)}, u32[]{:S(2)}) copy-start(f32[2,256,768]{2,1,0:T(8,128)} %copy-done.6) | copy-start | bytes 4718596
  215.4 6.5 %copy-start.17 = (bf16[2,256,3072]{2,1,0:T(8,128)(2,1)}, bf16[2,256,3072]{2,1,0:T(8,128)(2,1)S(1)}, u32[]{:S(2)}) copy-start(bf16[2,256,3072]{2,1,0:T(8,128)(2,1)S(1)} %get-tuple-element.50) | copy-start | bytes 9437188
  222.8 0.9 copy-start.10
  229.0 4.3 copy-start
  229.0 4.3 copy-start.12
  229.0 11.1 %slice-start.6 = ((s8[6291456]{0:T(1024)(128)(4,1)}), s8[4194304]{0:T(1024)(128)(4,1)S(1)}, s32[]{:S(2)}) async-start(s8[6291456]{0:T(1024)(128)(4,1)} %bitcast.125), calls=%async_computation.9 | async-start | bytes 8388608
  233.2 6.8 %slice-start.7 = ((s8[6291456]{0:T(1024)(128)(4,1)}), s8[2097152]{0:T(1024)(128)(4,1)S(1)}, s32[]{:S(2)}) async-start(s8[6291456]{0:T(1024)(128)(4,1)} %bitcast.125), calls=%async_computation.10 | async-start | bytes 4194304
  246.1 1.1 copy-start.3
  251.5 5.5 copy-start.11
  251.5 5.5 copy-start.14
  251.5 7.6 %copy-start.8 = (f32[2,256,768]{2,1,0:T(8,128)S(1)}, f32[2,256,768]{2,1,0:T(8,128)}, u32[]{:S(2)}) copy-start(f32[2,256,768]{2,1,0:T(8,128)} %copy-done.6) | copy-start | bytes 4718596
  251.5 7.6 %copy-start.18 = (bf16[2,256,3072]{2,1,0:T(8,128)(2,1)S(1)}, bf16[2,256,3072]{2,1,0:T(8,128)(2,1)}, u32[]{:S(2)}) copy-start(bf16[2,256,3072]{2,1,0:T(8,128)(2,1)} %copy-done.17) | copy-start | bytes 9437188
  304.4 12.3 %copy-start.4 = (f32[128,4608]{1,0:T(8,128)S(1)}, f32[128,4608]{1,0:T(8,128)}, u32[]{:S(2)}) copy-start(f32[128,4608]{1,0:T(8,128)} %reshape_reshape.13) | copy-start | bytes 7077892
  316.7 10.4 %slice-start = ((s8[9437184]{0:T(1024)(128)(4,1)}), s8[4194304]{0:T(1024)(128)(4,1)S(1)}, s32[]{:S(2)}) async-start(s8[9437184]{0:T(1024)(128)(4,1)} %bitcast.116), calls=%async_computation.3 | async-start | bytes 8388608
  318.4 8.8 %slice-start.1 = ((s8[9437184]{0:T(1024)(128)(4,1)}), s8[4194304]{0:T(1024)(128)(4,1)S(1)}, s32[]{:S(2)}) async-start(s8[9437184]{0:T(1024)(128)(4,1)} %bitcast.116), calls=%async_computation.4 | async-start | bytes 8388608
  318.4 8.8 %slice-start.2 = ((s8[9437184]{0:T(1024)(128)(4,1)}), s8[1048576]{0:T(1024)(128)(4,1)S(1)}, s32[]{:S(2)}) async-start(s8[9437184]{0:T(1024)(128)(4,1)} %bitcast.116), calls=%async_computation.5 | async-start | bytes 2097152
  382.2 1.9 copy-start.1
  382.2 1.9 copy-start.15
Sparse Core Ops, SparseCore 0:
  11.7 75.1 all-gather.6
  90.0 65.5 all-gather.4
  382.3 234.4 all-reduce.4
where the time goes:
time: 643 us; the launch traced here: 632 us
  waiting for transfers between devices  227 us (35%)
  local copies, waits for them, and re-layouts  146 us (23%)
  blocking collectives  125 us (19%)
  matrix products  78.8 us (12%)
  other arithmetic  40.3 us (6%)
  between operations  14.5 us (2%)
    unnamed x4, waiting for transfers between devices  227 us
    unnamed x1, blocking collectives  65 us
    all_gather x1, blocking collectives, in_one_piece(): lax.all_gather(both, axis, axis=dim, tiled=True)  59.9 us
    unnamed x72, local copies, waits for them, and re-layouts  47.6 us
    another operation x4, local copies, waits for them, and re-layouts, sum_packed(): lines = jnp.concatenate([b.reshape(count, -1) for b in tiles], axis=1)  32.9 us
    reshape x1, local copies, waits for them, and re-layouts, sum_packed(): jnp.pad(lines, ((0, 0), (0, extent * 128 - lines.shape[1])))  25.5 us
    pad x1, local copies, waits for them, and re-layouts, sum_packed(): jnp.pad(lines, ((0, 0), (0, extent * 128 - lines.shape[1])))  20.7 us
    convert_element_type x1, other arithmetic, forward(): activated = gelu_exact(up_pre).astype(jnp.bfloat16)  15.9 us
  transfers between devices with their start and end apart: 3, of which 1 were waited for; matrix products, arithmetic and copies ran while one was open for 12% of the time, Pallas kernels for 0%

commit v1 on v0

v1 whole, which is shorter than its diff:
```python
import functools

import jax
import jax.numpy as jnp
import numpy as np
from jax import lax
from jax.experimental import pallas as pl
from jax.experimental.pallas import tpu as pltpu
from jax.sharding import Mesh, PartitionSpec as P

B16 = jnp.bfloat16
F32 = jnp.float32
HEADS = 12
HEAD_DIM = 64
D = 768
FF = 3072
LEN = 256
HALF = 128
ROWS = 512
PAD = 1024
CHUNK = 512
SCALE = HEAD_DIM**-0.5
ALL = ("x", "core", "y", "z")
SIZES = (4, 2, 4, 4)
VMEM = 60 * 1024 * 1024
RSQRT2 = 0.5**0.5
RSQRT2PI = (2.0 * np.pi) ** -0.5


def dot(a, b, ca=1, cb=0):
    return lax.dot_general(a, b, (((ca,), (cb,)), ((), ())), preferred_element_type=F32)


def pick(a, p):
    return dot(a, p).astype(B16)


def put_back(a, p):
    high = a.astype(B16)
    rest = (a - high.astype(F32)).astype(B16)
    return dot(high, p, 1, 1) + dot(rest, p, 1, 1)


def norm_stats(v):
    centered = v - jnp.mean(v, axis=-1, keepdims=True)
    variance = jnp.mean(centered * centered, axis=-1, keepdims=True)
    scale = lax.rsqrt(variance + 1e-05)
    return centered * scale, scale


def norm_back(grad, hat, scale, gain):
    g = grad * gain
    mean_g = jnp.mean(g, axis=-1, keepdims=True)
    mean_gh = jnp.mean(g * hat, axis=-1, keepdims=True)
    return scale * (g - mean_g - hat * mean_gh)


def row_sum(v):
    return jnp.sum(v, axis=0, keepdims=True)


def softmax_of(q_one, k_two, valid):
    s = jnp.where(valid, dot(q_one, k_two, 1, 1), -1000000000.0)
    e = jnp.exp(s - jnp.max(s, axis=-1, keepdims=True))
    return e / jnp.sum(e, axis=-1, keepdims=True)


def attention_kernel(
    lens_ref, x_ref, wqk_ref, wv_ref, wo_ref, ext_ref, py_ref, pz_ref, spread_ref,
    a1_ref, qkv_ref, o_ref, x1_ref, a2_ref, par_ref, ub_ref,
):
    par = dot(ext_ref[...], py_ref[...], 0, 1)
    par_ref[...] = par[:8]
    lane = lax.broadcasted_iota(jnp.int32, (8, PAD), 1) % 8
    own = lane == lax.broadcasted_iota(jnp.int32, (8, PAD), 0)
    for j in range(3):
        wide = dot(par[8 + 8 * j : 16 + 8 * j].astype(B16), spread_ref[...])
        ub_ref[j : j + 1, :] = row_sum(jnp.where(own, wide, 0.0))
    ub_ref[3:, :] = jnp.zeros((5, PAD), F32)
    x = x_ref[...].astype(F32)
    hat, _ = norm_stats(x)
    a1 = (hat * par[0:1] + par[2:3]).astype(B16)
    a1_ref[...] = a1
    qk = dot(pick(a1, py_ref[...]), wqk_ref[...])
    qkv_ref[:, :D] = (qk[:, :D] + par[3:4]).astype(B16)
    qkv_ref[:, D : 2 * D] = qk[:, D:].astype(B16)
    qkv_ref[:, 2 * D :] = (dot(pick(a1, pz_ref[...]), wv_ref[...]) + par[4:5]).astype(B16)
    head_lane = lax.broadcasted_iota(jnp.int32, (LEN, 128), 1) < HEAD_DIM
    key = lax.broadcasted_iota(jnp.int32, (1, LEN), 1)
    for cell in range(2):
        valid = key < lens_ref[cell]
        rows = slice(cell * LEN, (cell + 1) * LEN)
        for pair in range(HEADS // 2):
            at = pair * 128
            q = qkv_ref[rows, at : at + 128] * SCALE
            k = qkv_ref[rows, D + at : D + at + 128]
            v = qkv_ref[rows, 2 * D + at : 2 * D + at + 128]
            total = None
            for head in range(2):
                mine = head_lane if head == 0 else ~head_lane
                p = softmax_of(jnp.where(mine, q, 0), k, valid).astype(B16)
                o = dot(p, jnp.where(mine, v, 0))
                total = o if total is None else total + o
            o_ref[rows, at : at + 128] = total.astype(B16)
    x1 = x + dot(pick(o_ref[...], pz_ref[...]), wo_ref[...]) + par[5:6]
    hat, _ = norm_stats(x1)
    a2 = (hat * par[1:2] + par[6:7]).astype(B16)
    for cell in range(2):
        for half in range(2):
            src = slice(cell * LEN + half * HALF, cell * LEN + (half + 1) * HALF)
            dst = slice(half * LEN + cell * HALF, half * LEN + (cell + 1) * HALF)
            x1_ref[dst, :] = x1[src]
            a2_ref[dst, :] = a2[src]


def ffn_kernel(
    offs_ref, a2_ref, x1_ref, pos_ref, cot_ref, par_ref, ub_ref, py_ref, pz_ref,
    gy_ref, gz_ref, yz_ref, wup_ref, wdn_ref,
    mixed_ref, dx1_ref, vec_ref, ubg_ref, yk_ref, ys_ref, zk_ref, zs_ref, dk_ref, ds_ref,
    a2f, a2g, dy, dz, acc, dacc, g_all,
):
    c = pl.program_id(0)

    @pl.when(c == 0)
    def _():
        a2 = a2_ref[...]
        a2f[0] = pick(a2, py_ref[...])
        a2f[1] = pick(a2, pz_ref[...])
        a2g[0] = pick(a2[:LEN], gy_ref[...])
        a2g[1] = pick(a2[:LEN], gz_ref[...])
        row = lax.broadcasted_iota(jnp.int32, (HALF, 64), 0)
        for cell in range(2):
            hot = (row == pos_ref[cell : cell + 1, :]).astype(F32).astype(B16)
            part = dot(hot, cot_ref[cell])
            dy[cell * HALF : (cell + 1) * HALF, :] = part
            dz[cell * HALF : (cell + 1) * HALF, :] = part.astype(B16)
        acc[...] = jnp.zeros_like(acc)
        dacc[...] = jnp.zeros_like(dacc)

    lane = c // 3
    wup = wup_ref[...]
    wdn = wdn_ref[...]
    u = dot(a2f[lane], wup) + ub_ref[pl.ds(c // 2, 1), pl.ds((c % 2) * CHUNK, CHUNK)]
    phi = 0.5 + 0.5 * lax.erf(u * RSQRT2)
    g = (u * phi).astype(B16)
    acc[...] += dot(g, wdn)
    top = u[:LEN]
    slope = phi[:LEN] + top * (jnp.exp(-0.5 * top * top) * RSQRT2PI)
    du_wide = dot(dz[...], wdn, 1, 1) * slope
    du = du_wide.astype(B16)
    dacc[lane] += dot(du, wup, 1, 1)
    ubg_ref[pl.ds(c // 2, 1), pl.ds((c % 2) * CHUNK, CHUNK)] = row_sum(du.astype(F32))
    dw = dot(a2g[lane], du, 0, 0).astype(B16)

    @pl.when(c < 3)
    def _():
        yk_ref[...] = dw[:384]
        ys_ref[...] = dw[384:]

    @pl.when(c >= 3)
    def _():
        zk_ref[...] = dw[:384]
        zs_ref[...] = dw[384:]

    g_all[:, pl.ds(pl.multiple_of((c % 2) * CHUNK, CHUNK), CHUNK)] = g[:LEN]

    @pl.when(c % 2 == 1)
    def _():
        for half, out in ((0, dk_ref), (1, ds_ref)):
            blocks = []
            for i in range(4):
                at = pl.multiple_of(offs_ref[half * 4 + i] * 128, 128)
                blocks.append(pick(g_all[:, pl.ds(at, 128)], yz_ref[half]))
            grad = dot(jnp.concatenate(blocks, axis=1), dz[...], 0, 0).astype(B16)
            for i in range(4):
                at = pl.multiple_of(i * 384 + (c // 2) * 128, 128)
                out[pl.ds(at, 128), :] = grad[i * 128 : (i + 1) * 128]

    @pl.when(c == 5)
    def _():
        x1 = x1_ref[...]
        mixed = (x1 + acc[...] + par_ref[7:8]).astype(B16)
        for cell in range(2):
            for half in range(2):
                dst = slice(cell * LEN + half * HALF, cell * LEN + (half + 1) * HALF)
                src = slice(half * LEN + cell * HALF, half * LEN + (cell + 1) * HALF)
                mixed_ref[dst, :] = mixed[src]
        da2 = put_back(dacc[0], py_ref[...]) + put_back(dacc[1], pz_ref[...])
        hat, scale = norm_stats(x1[:LEN])
        dx1_ref[...] = dy[...] + norm_back(da2, hat, scale, par_ref[1:2])
        vec_ref[0:1, :] = row_sum(da2 * hat)
        vec_ref[1:2, :] = row_sum(da2)
        vec_ref[2:3, :] = row_sum(dz[...].astype(F32))
        vec_ref[3:, :] = jnp.zeros((5, D), F32)
        ubg_ref[3:, :] = jnp.zeros((5, PAD), F32)


def attention_back_kernel(
    lens_ref, dx1_ref, o_ref, qkv_ref, wo_ref, pz_ref, gz_ref,
    ok_ref, os_ref, dq_ref, dk_ref, dv_ref, vec_ref, do_ref,
):
    db = dx1_ref[...].astype(B16)
    do_ref[...] = pick(dot(db, wo_ref[...], 1, 1).astype(B16), pz_ref[...].T)
    o = jnp.concatenate([o_ref[:HALF], o_ref[LEN : LEN + HALF]], axis=0)
    grad = dot(pick(o, gz_ref[...]), db, 0, 0).astype(B16)
    ok_ref[...] = grad[:384]
    os_ref[...] = grad[384:]
    head_lane = lax.broadcasted_iota(jnp.int32, (LEN, 128), 1) < HEAD_DIM
    key = lax.broadcasted_iota(jnp.int32, (1, LEN), 1)
    for cell in range(2):
        valid = key < lens_ref[cell]
        rows = slice(cell * LEN, (cell + 1) * LEN)
        first = slice(cell * LEN, cell * LEN + HALF)
        grads = slice(cell * HALF, (cell + 1) * HALF)
        for pair in range(HEADS // 2):
            at = pair * 128
            q = qkv_ref[first, at : at + 128] * SCALE
            k = qkv_ref[rows, D + at : D + at + 128]
            v = qkv_ref[rows, 2 * D + at : 2 * D + at + 128]
            do = do_ref[grads, at : at + 128]
            dq = dk = dv = None
            for head in range(2):
                mine = head_lane if head == 0 else ~head_lane
                q_one = jnp.where(mine[:HALF], q, 0)
                do_one = jnp.where(mine[:HALF], do, 0)
                p = softmax_of(q_one, k, valid)
                dp = dot(do_one, v, 1, 1)
                ds = (p * (dp - jnp.sum(dp * p, axis=-1, keepdims=True))).astype(B16)
                dq_h = dot(ds, jnp.where(mine, k, 0))
                dk_h = dot(ds, q_one, 0, 0)
                dv_h = dot(p.astype(B16), do_one, 0, 0)
                dq = dq_h if dq is None else dq + dq_h
                dk = dk_h if dk is None else dk + dk_h
                dv = dv_h if dv is None else dv + dv_h
            dq_ref[grads, at : at + 128] = (dq * SCALE).astype(B16)
            dk_ref[rows, at : at + 128] = dk.astype(B16)
            dv_ref[rows, at : at + 128] = dv.astype(B16)
    vec_ref[0:1, :] = row_sum(db.astype(F32))
    vec_ref[1:2, :] = row_sum(dq_ref[...].astype(F32))
    vec_ref[2:3, :] = row_sum(dv_ref[...].astype(F32))
    vec_ref[3:, :] = jnp.zeros((5, D), F32)


def qkv_grad_kernel(
    a1_ref, dq_ref, dk_ref, dv_ref, gy_ref, gz_ref, qkk_ref, qks_ref, vk_ref, vs_ref
):
    a1 = a1_ref[...]
    a1y = pick(a1, gy_ref[...])
    a1z = pick(a1, gz_ref[...])
    a1q = jnp.concatenate([a1y[:HALF], a1y[LEN : LEN + HALF]], axis=0)
    grad_q = dot(a1q, dq_ref[...], 0, 0).astype(B16)
    qkk_ref[:, :D] = grad_q[:384]
    qks_ref[:, :D] = grad_q[384:]
    grad_k = dot(a1y, dk_ref[...], 0, 0).astype(B16)
    qkk_ref[:, D:] = grad_k[:384]
    qks_ref[:, D:] = grad_k[384:]
    grad_v = dot(a1z, dv_ref[...], 0, 0).astype(B16)
    vk_ref[...] = grad_v[:384]
    vs_ref[...] = grad_v[384:]


def input_grad_kernel(
    dq_ref, dk_ref, dv_ref, wqk_ref, wv_ref, py_ref, pz_ref, gy_ref, spread_ref,
    x_ref, dx1_ref, par_ref, vec_b_ref, vec_c_ref, ubg_ref,
    out_ref, ek_ref, es_ref, da_ref,
):
    from_q = put_back(dot(dq_ref[...], wqk_ref[:, :D], 1, 1), py_ref[...])
    da_ref[...] = put_back(dot(dk_ref[...], wqk_ref[:, D:], 1, 1), py_ref[...])
    da_ref[...] += put_back(dot(dv_ref[...], wv_ref[...], 1, 1), pz_ref[...])
    for cell in range(2):
        first = slice(cell * LEN, cell * LEN + HALF)
        da_ref[first, :] += from_q[cell * HALF : (cell + 1) * HALF]
    da = da_ref[...]
    hat, scale = norm_stats(x_ref[...].astype(F32))
    out_ref[...] = norm_back(da, hat, scale, par_ref[0:1])
    for cell in range(2):
        first = slice(cell * LEN, cell * LEN + HALF)
        out_ref[first, :] += dx1_ref[cell * HALF : (cell + 1) * HALF]
    lane = lax.broadcasted_iota(jnp.int32, (8, PAD), 1) % 8
    own = lane == lax.broadcasted_iota(jnp.int32, (8, PAD), 0)
    lines = [
        row_sum(da * hat), vec_b_ref[0:1], row_sum(da), vec_c_ref[1:2],
        vec_c_ref[2:3], vec_c_ref[0:1], vec_b_ref[1:2], vec_b_ref[2:3],
    ]
    for j in range(3):
        part = jnp.where(own, ubg_ref[j : j + 1, :], 0.0).astype(B16)
        lines.append(dot(part, spread_ref[...], 1, 1))
    lines.append(jnp.zeros((96, D), F32))
    vecs = jnp.concatenate(lines, axis=0).astype(B16)
    ext = dot(gy_ref[...], vecs, 0, 1).astype(B16)
    ek_ref[...] = ext[:384]
    es_ref[...] = ext[384:]


def whole(kernel, outs, flops, scratch=(), smem=0):
    def call(*args):
        specs = [pl.BlockSpec(memory_space=pltpu.SMEM)] * smem
        specs += [pl.BlockSpec(memory_space=pltpu.VMEM)] * (len(args) - smem)
        size = sum(a.size * a.dtype.itemsize for a in (*args, *outs))
        return pl.pallas_call(
            kernel,
            out_shape=outs,
            in_specs=specs,
            out_specs=[pl.BlockSpec(memory_space=pltpu.VMEM)] * len(outs),
            scratch_shapes=scratch,
            compiler_params=pltpu.CompilerParams(vmem_limit_bytes=VMEM),
            cost_estimate=pl.CostEstimate(flops=flops, bytes_accessed=size, transcendentals=0),
        )(*args)

    return call


def shape(*dims, dtype=B16):
    return jax.ShapeDtypeStruct(dims, dtype)


def swap_list(axis, step):
    pairs = []
    for flat in range(128):
        at = list(np.unravel_index(flat, SIZES))
        if axis == "core":
            at[1] ^= 1
        else:
            at[ALL.index(axis)] ^= 3 if (at[1] + step) % 2 else 1
        pairs.append((flat, int(np.ravel_multi_index(at, SIZES))))
    return pairs


def swap(v, axis, step=0):
    return lax.ppermute(v, ALL, swap_list(axis, step))


def relative(core, own):
    even = jnp.array([0, 1, 3, 2], jnp.int32)
    odd = jnp.array([0, 3, 1, 2], jnp.int32)
    return own ^ jnp.where(core == 0, even, odd)


def positions_of(at, order):
    total = 0
    core = jnp.stack([at["core"], 1 - at["core"]])
    weight = {"x": 32, "core": 16, "y": 4, "z": 1}
    total = core.reshape(2, 1, 1, 1, 1) * weight["core"] * 6
    for i, axis in enumerate(order):
        dims = [2, 1, 1, 1, 1]
        dims[1 + i] = 4
        rel = jnp.stack([relative(at["core"], at[axis]), relative(1 - at["core"], at[axis])])
        total = total + rel.reshape(dims) * weight[axis] * 6
    total = total + jnp.arange(6, dtype=jnp.int32)
    return total.reshape(D)


def one_hot(count, at):
    return (jnp.arange(count, dtype=jnp.int32)[:, None] == at[None, :]).astype(B16)


def halve(own, got, axis):
    for step in range(2):
        half = own.shape[0] // 2
        send = (own[half:] + got[half:].astype(F32)).astype(B16)
        keep = own[:half] + got[:half].astype(F32)
        own, got = keep, swap(send, axis, step=1 - step)
    return own, got


def local(
    tokens, lengths, positions, cotangent, qkv_weight, out_weight, up_weight, down_weight,
    norm_gains, biases, up_bias,
):
    at = {a: lax.axis_index(a) for a in ALL}
    lane_y = one_hot(D, positions_of(at, ("y", "z", "x")))
    lane_z = one_hot(D, positions_of(at, ("z", "x", "y")))
    eights = jnp.arange(PAD, dtype=jnp.int32)
    padded = one_hot(D, jnp.where(eights % 8 < 6, eights // 8 * 6 + eights % 8, -1))
    spread = one_hot(D, eights // 8 * 6)
    inner, offs = [], []
    for core in (at["core"], 1 - at["core"]):
        y = relative(core, at["y"]).reshape(4, 1, 1)
        z = relative(core, at["z"]).reshape(1, 4, 1)
        inner.append(one_hot(128, (y * 32 + z * 8 + jnp.arange(8, dtype=jnp.int32)).reshape(128)))
        offs.append(relative(core, at["x"]) * 2 + core)
    inner, offs = jnp.stack(inner), jnp.concatenate(offs)

    ub = jnp.zeros((6, 24), B16).at[0].set(up_bias.reshape(8, 3).T.reshape(24))
    ext = jnp.concatenate([norm_gains.T, biases.T, ub, jnp.zeros((6, 96), B16)], axis=1)
    up = up_weight.reshape(6, PAD, 3).transpose(0, 2, 1).reshape(6, FF)
    shard = jnp.concatenate([qkv_weight, out_weight, up], axis=1)
    shard = jnp.pad(shard, ((0, 2), (0, 0)))
    ext = jnp.pad(ext, ((0, 2), (0, 0)))
    shard = jnp.concatenate([shard, down_weight.reshape(8, 3 * D), ext], axis=1)
    full = lax.all_gather(shard, ALL, axis=0, tiled=True)
    wqk, wv, wo = full[:, : 2 * D], full[:, 2 * D : 3 * D], full[:, 3 * D : 4 * D]
    ext_all = full[:, 8448:]
    py = pz = padded

    x = tokens.reshape(ROWS, D)
    a1, qkv, o, x1, a2, par, ubw = whole(
        attention_kernel,
        [shape(ROWS, D), shape(ROWS, 3 * D), shape(ROWS, D), shape(ROWS, D, dtype=F32),
         shape(ROWS, D), shape(8, D, dtype=F32), shape(8, PAD, dtype=F32)],
        7_000_000_000, smem=1,
    )(lengths, x, wqk, wv, wo, ext_all, py, pz, spread)

    kp = py.shape[1]
    fixed = lambda *dims: pl.BlockSpec(dims, lambda c: (0,) * len(dims))
    mixed, dx1, vec_b, ubg, yk, ys, zk, zs, dnk, dns = pl.pallas_call(
        ffn_kernel,
        grid=(6,),
        in_specs=[
            pl.BlockSpec(memory_space=pltpu.SMEM),
            fixed(ROWS, D), fixed(ROWS, D), fixed(2, 64), fixed(2, 64, D), fixed(8, D), fixed(8, PAD),
            fixed(D, kp), fixed(D, kp), fixed(D, D), fixed(D, D), fixed(2, 128, 128),
            pl.BlockSpec((kp, CHUNK), lambda c: (0, 6 + c)),
            pl.BlockSpec((CHUNK, D), lambda c: (c % 2, 8 + c // 2)),
        ],
        out_specs=[
            fixed(ROWS, D), fixed(LEN, D), fixed(8, D), fixed(8, PAD),
            pl.BlockSpec((384, CHUNK), lambda c: (0, jnp.minimum(c, 2))),
            pl.BlockSpec((384, CHUNK), lambda c: (0, jnp.minimum(c, 2))),
            pl.BlockSpec((384, CHUNK), lambda c: (0, jnp.maximum(c - 3, 0))),
            pl.BlockSpec((384, CHUNK), lambda c: (0, jnp.maximum(c - 3, 0))),
            fixed(1536, D), fixed(1536, D),
        ],
        out_shape=[
            shape(ROWS, D), shape(LEN, D, dtype=F32), shape(8, D, dtype=F32), shape(8, PAD, dtype=F32),
            shape(384, 1536), shape(384, 1536), shape(384, 1536), shape(384, 1536),
            shape(1536, D), shape(1536, D),
        ],
        scratch_shapes=[
            pltpu.VMEM((2, ROWS, kp), B16), pltpu.VMEM((2, LEN, D), B16), pltpu.VMEM((LEN, D), F32),
            pltpu.VMEM((LEN, D), B16), pltpu.VMEM((ROWS, D), F32), pltpu.VMEM((2, LEN, kp), F32),
            pltpu.VMEM((LEN, PAD), B16),
        ],
        compiler_params=pltpu.CompilerParams(vmem_limit_bytes=VMEM),
        cost_estimate=pl.CostEstimate(flops=10_000_000_000, bytes_accessed=30_000_000, transcendentals=0),
    )(offs, a2, x1, positions, cotangent, par, ubw, py, pz, lane_y, lane_z, inner, full, full)

    got = swap(dns, "core")
    own, got = halve(dnk.astype(F32), got, "x")
    own, got = own.reshape(3, 128, D), got.reshape(3, 128, D)
    for axis in ("y", "z"):
        for step in range(2):
            half = own.shape[1] // 2
            send = (own[:, half:] + got[:, half:].astype(F32)).astype(B16)
            own = own[:, :half] + got[:, :half].astype(F32)
            got = swap(send, axis, step=1 - step)
    down_grad = (own + got.astype(F32)).transpose(1, 0, 2).reshape(24, D)

    got_y, got_z = swap(ys, "core"), swap(zs, "core")
    y2 = halve(yk.astype(F32), got_y, "y")
    z2 = halve(zk.astype(F32), got_z, "z")

    ok, os, dq, dk, dv, vec_c = whole(
        attention_back_kernel,
        [shape(384, D), shape(384, D), shape(LEN, D), shape(ROWS, D), shape(ROWS, D), shape(8, D, dtype=F32)],
        5_000_000_000, scratch=[pltpu.VMEM((LEN, D), B16)], smem=1,
    )(lengths, dx1, o, qkv, wo, pz, lane_z)
    got_o = swap(os, "core")
    qkk, qks, vk, vs = whole(
        qkv_grad_kernel,
        [shape(384, 2 * D), shape(384, 2 * D), shape(384, D), shape(384, D)],
        3_000_000_000,
    )(a1, dq, dk, dv, lane_y, lane_z)
    got_qk, got_v = swap(qks, "core"), swap(vs, "core")
    token_grad, ek, es = whole(
        input_grad_kernel,
        [shape(ROWS, D, dtype=F32), shape(384, 128), shape(384, 128)],
        4_000_000_000, scratch=[pltpu.VMEM((ROWS, D), F32)],
    )(dq, dk, dv, wqk, wv, py, pz, lane_y, spread, x, dx1, par, vec_b, vec_c, ubg)
    got_e = swap(es, "core")

    wide = lambda *parts: jnp.concatenate(parts, axis=1)
    y1 = halve(wide(qkk, ek).astype(F32), wide(got_qk, got_e), "y")
    z1 = halve(wide(vk, ok).astype(F32), wide(got_v, got_o), "z")

    own, got = halve(wide(y2[0], y1[0]), wide(y2[1], y1[1]), "z")
    own, got = halve(own, got, "x")
    y_sum = own + got.astype(F32)
    own, got = halve(wide(z2[0], z1[0]), wide(z2[1], z1[1]), "x")
    own, got = halve(own, got, "y")
    z_sum = own + got.astype(F32)

    up_grad = wide(y_sum[:, :1536], z_sum[:, :1536])
    up_grad = up_grad.reshape(6, 3, PAD).transpose(0, 2, 1).reshape(6, FF)
    qkv_grad = wide(y_sum[:, 1536:3072], z_sum[:, 1536:2304])
    out_grad = z_sum[:, 2304:]
    small = y_sum[:, 3072:]
    gains_grad, biases_grad = small[:, 0:2].T, small[:, 2:8].T
    up_bias_grad = small[0, 8:32].reshape(3, 8).T.reshape(24)
    return (
        mixed.reshape(2, LEN, D), token_grad.reshape(2, LEN, D), qkv_grad, out_grad, up_grad, down_grad,
        gains_grad, biases_grad, up_bias_grad,
    )


def solution(mesh):
    fine = Mesh(mesh.devices.reshape(SIZES), ALL)
    rows = lambda n: P(ALL, *([None] * (n - 1)))
    cols = P(None, ALL)
    in_specs = (rows(3), rows(1), rows(2), rows(3), rows(2), rows(2), rows(2), rows(2), cols, cols, rows(1))
    out_specs = (rows(3), rows(3), rows(2), rows(2), rows(2), rows(2), cols, cols, rows(1))
    return jax.shard_map(local, mesh=fine, in_specs=in_specs, out_specs=out_specs, check_vma=False)
```

time: 643 us -> 318 us (0.49); the launches traced: 632 us -> 315 us
  blocking collectives: 125 us -> 0 us
  local copies, waits for them, and re-layouts: 146 us -> 30.4 us
  waiting for transfers between devices: 227 us -> 133 us
  Pallas kernels: 0 us -> 82.8 us
  matrix products: 78.8 us -> 0 us
  starting transfers between devices: 0.12 us -> 35.9 us
  other arithmetic: 40.3 us -> 18.2 us
    unnamed x4 -> x1, waiting for transfers between devices: 227 us -> 0.02 us
    pallas_call x0 -> x5, Pallas kernels: none -> 82.8 us  [the longest x4 52.9 us: call(): pl.pallas_call(kernel, out_shape=outs, in_specs=specs, out_specs=[pl.Bloc...]
    dot_general x18 -> x0, matrix products: 78.8 us -> none  [the longest x1 9.02 us: backward(): jnp.einsum('cld,fd->clf', down_in, down_weight, preferred_element_type=jn...]
    all_gather x2 -> x1, waiting for transfers between devices: 0.01 us -> 74.7 us  [local(): full = lax.all_gather(shard, ALL, axis=0, tiled=True)]
    unnamed x1 -> x0, blocking collectives: 65 us -> none
    all_gather x1 -> x0, blocking collectives: 59.9 us -> none  [in_one_piece(): lax.all_gather(both, axis, axis=dim, tiled=True)]
    ppermute x0 -> x29, waiting for transfers between devices: none -> 58.3 us  [swap(): return lax.ppermute(v, ALL, swap_list(axis, step))]
    unnamed x72 -> x39, local copies, waits for them, and re-layouts: 47.6 us -> 7.9 us
  transfers between devices with their start and end apart: 3 -> 30, of which waited for: 1 -> 15; matrix products, arithmetic and copies ran while one was open for 12% -> 7% of each run, Pallas kernels for 0% -> 0%
where the time goes in v1:
time: 318 us; the launch traced here: 315 us
  waiting for transfers between devices  133 us (42%)
  Pallas kernels  82.8 us (26%)
  starting transfers between devices  35.9 us (11%)
  local copies, waits for them, and re-layouts  30.4 us (10%)
  other arithmetic  18.2 us (6%)
  between operations  14.8 us (5%)
    all_gather x1, waiting for transfers between devices, local(): full = lax.all_gather(shard, ALL, axis=0, tiled=True)  74.7 us
    ppermute x29, waiting for transfers between devices, swap(): return lax.ppermute(v, ALL, swap_list(axis, step))  58.3 us
    pallas_call x4, Pallas kernels, call(): pl.pallas_call(kernel, out_shape=outs, in_specs=specs, out_specs=[pl.Bloc...  52.9 us
    ppermute x29, starting transfers between devices, swap(): return lax.ppermute(v, ALL, swap_list(axis, step))  35.9 us
    pallas_call x1, Pallas kernels, local(): pl.pallas_call(ffn_kernel, grid=(6,), in_specs=[pl.BlockSpec(memory_space...  30 us
    unnamed x39, local copies, waits for them, and re-layouts  7.9 us
    slice x2, local copies, waits for them, and re-layouts, local(): wqk, wv, wo = (full[:, :2 * D], full[:, 2 * D:3 * D], full[:, 3 * D:4 * D])  7.63 us
  transfers between devices with their start and end apart: 30, of which 15 were waited for; matrix products, arithmetic and copies ran while one was open for 7% of the time, Pallas kernels for 0%

profile of v1, /device:TPU:32, one launch (start us, length us, event | category | flops | bytes accessed | tf_op | source)
XLA Modules:
  0.0 315.1 jit_solution(810359948644728709)
XLA Ops:
  10.5 4.1 %reshape.501 = bf16[6,1024,3]{2,1,0:T(8,128)(2,1)S(1)} reshape(bf16[6,3072]{1,0:T(8,128)(2,1)} %param.55) | data formatting | bytes 73728 | tf_op jit(solution)/shard_map/reshape | solution.py:386
  22.3 2.9 fusion
  25.2 74.7 %all-gather.2.cloned.1.call-done.wup_ref.wdn_ref = bf16[1024,8576]{1,0:T(8,128)(2,1)} async-done(((bf16[8,8576]{1,0:T(8,128)(2,1)}), bf16[1024,8576]{1,0:T(8,128)(2,1)}) %all-gather.2.cloned.1.call-update) | async-done | bytes 17563664 | tf_op jit(solution)/shard_map/all_gather | solution.py:391
  101.6 3.8 %slice.418.wqk_ref = bf16[1024,1536]{1,0:T(8,128)(2,1)} slice(bf16[1024,8576]{1,0:T(8,128)(2,1)} %all-gather.2.cloned.1.call-done.wup_ref.wdn_ref), slice={[0:1024], [0:1536]} | slice | bytes 6291456 | tf_op jit(solution)/shard_map/slice | solution.py:392
  105.4 3.9 %fusion.58 = (bf16[1024,768]{1,0:T(8,128)(2,1)}, bf16[1024,768]{1,0:T(8,128)(2,1)}) fusion(bf16[1024,8576]{1,0:T(8,128)(2,1)} %all-gather.2.cloned.1.call-done.wup_ref.wdn_ref), kind=kLoop, calls=%fused_computation.165 | loop fusion | bytes 6291456 | tf_op jit(solution)/shard_map/slice | solution.py:392
  109.2 18.7 %shard_map.502 = (bf16[512,768]{1,0:T(8,128)(2,1)}, bf16[512,2304]{1,0:T(8,128)(2,1)}, bf16[512,768]{1,0:T(8,128)(2,1)}, f32[512,768]{1,0:T(8,128)}, bf16[512,76...) custom-call(s32[2]{0:T(128)} %lens_ref.3, bf16[512,768]{1,0:T(8,128)(2,1)} %bitcast.43, ...), custom_call_target="tpu_custom_call" | custom-call | flops 7000000000 | bytes 18407432 | tf_op jit(solution)/shard_map/pallas_call | solution.py:300
  127.9 30.0 %shard_map.503 = (bf16[512,768]{1,0:T(8,128)(2,1)}, f32[256,768]{1,0:T(8,128)}, f32[8,768]{1,0:T(8,128)}, f32[8,1024]{1,0:T(8,128)}, bf16[384,1536]{1,0:T(8,128)...) custom-call(s32[8]{0:T(128)} %pad_add_fusion.offs_ref, ...), custom_call_target="tpu_custom_call" | custom-call | flops 10000000000 | bytes 30000000 | tf_op jit(solution)/shard_map/pallas_call | solution.py:406
  157.9 13.2 %shard_map.504 = (bf16[384,768]{1,0:T(8,128)(2,1)}, bf16[384,768]{1,0:T(8,128)(2,1)}, bf16[256,768]{1,0:T(8,128)(2,1)}, bf16[512,768]{1,0:T(8,128)(2,1)}, bf16[512,768]{1,0:T(8,128)(2,1)}, /*index=5*/f32[8,768]{1,0:T(8,128)}) custom-call(s32[2]{0:T(128)} %lens_ref.3, f32[256,768]{1,0:T(8,128)} %get-tuple-element.56.dx1_ref, ...), custom_call_target="tpu_custom_call" | custom-call | flops 5000000000 | bytes 11427848 | tf_op jit(solution)/shard_map/pallas_call | solution.py:300
  171.0 6.6 %shard_map.506 = (bf16[384,1536]{1,0:T(8,128)(2,1)}, bf16[384,1536]{1,0:T(8,128)(2,1)}, bf16[384,768]{1,0:T(8,128)(2,1)}, bf16[384,768]{1,0:T(8,128)(2,1)}) custom-call(bf16[512,768]{1,0:T(8,128)(2,1)} %get-tuple-element.68.a1_ref, bf16[256,768]{1,0:T(8,128)(2,1)} %get-tuple-element.59.dq_ref, bf16[512,768]{1,0:T(8,128)(2,1)} %get-tuple-element.60.dk_ref, ...), custom_call_target="tpu_custom_call" | custom-call | flops 3000000000 | bytes 8650752 | tf_op jit(solution)/shard_map/pallas_call | solution.py:300
  177.7 14.4 %shard_map.505 = (f32[512,768]{1,0:T(8,128)}, bf16[384,128]{1,0:T(8,128)(2,1)}, bf16[384,128]{1,0:T(8,128)(2,1)}) custom-call(bf16[256,768]{1,0:T(8,128)(2,1)} %get-tuple-element.59.dq_ref, bf16[512,768]{1,0:T(8,128)(2,1)} %get-tuple-element.60.dk_ref, bf16[512,768]{1,0:T(8,128)(2,1)} %get-tuple-element.61.dv_ref, bf16[1024,1536]{1,0:T(8,128)(2,1)} %slice.418.wqk_ref, ...), custom_call_target="tpu_custom_call" | custom-call | flops 4000000000 | bytes 16031744 | tf_op jit(solution)/shard_map/pallas_call | solution.py:300
  203.7 2.8 collective-permute-start.4
  208.2 3.3 %collective-permute-done.15 = bf16[192,1536]{1,0:T(8,128)(2,1)S(1)} collective-permute-done((bf16[192,1536]{1,0:T(8,128)(2,1)S(1)}, bf16[192,1536]{1,0:T(8,128)(2,1)S(1)}, u32[]{:S(2)}, u32[]{:S(2)}) %collective-permute-start.15) | collective-permute-done | bytes 589856 | tf_op jit(solution)/shard_map/ppermute | solution.py:330
  211.7 2.3 collective-permute-start.17
  213.9 7.7 %collective-permute-done.1 = bf16[192,1536]{1,0:T(8,128)(2,1)S(1)} collective-permute-done((bf16[192,1536]{1,0:T(8,128)(2,1)S(1)}, bf16[192,1536]{1,0:T(8,128)(2,1)S(1)}, u32[]{:S(2)}, u32[]{:S(2)}) %collective-permute-start.1) | collective-permute-done | bytes 589856 | tf_op jit(solution)/shard_map/ppermute | solution.py:330
  222.3 1.9 collective-permute-start.16
  224.4 1.8 collective-permute-start.6
  226.2 2.9 collective-permute-done.16
  229.3 1.8 collective-permute-start.18
  232.7 4.5 %collective-permute-done.18 = bf16[48,3072]{1,0:T(8,128)(2,1)S(1)} collective-permute-done((bf16[48,3072]{1,0:T(8,128)(2,1)S(1)}, bf16[48,3072]{1,0:T(8,128)(2,1)S(1)}, u32[]{:S(2)}, u32[]{:S(2)}) %collective-permute-start.18) | collective-permute-done | bytes 294944 | tf_op jit(solution)/shard_map/ppermute | solution.py:330
  240.2 4.2 %collective-permute-done.19 = bf16[24,3072]{1,0:T(8,128)(2,1)S(1)} collective-permute-done((bf16[24,3072]{1,0:T(8,128)(2,1)S(1)}, bf16[24,3072]{1,0:T(8,128)(2,1)S(1)}, u32[]{:S(2)}, u32[]{:S(2)}) %collective-permute-start.19) | collective-permute-done | bytes 147488 | tf_op jit(solution)/shard_map/ppermute | solution.py:330
  244.5 3.6 %collective-permute-start.20 = (bf16[12,3072]{1,0:T(8,128)(2,1)S(1)}, bf16[12,3072]{1,0:T(8,128)(2,1)S(1)}, u32[]{:S(2)}, u32[]{:S(2)}) collective-permute-start(bf16[12,3072]{1,0:T(8,128)(2,1)S(1)} %get-tuple-element.139), channel_id=1, source_target_pairs={{0,12},{1,13},{2,14},{3,15},{4,8},{5,9},{6,10},{7,11},{8,4},{9,5},... | collective-permute-start | bytes 221192 | tf_op jit(solution)/shard_map/ppermute | solution.py:330
  248.2 2.2 collective-permute-start.8
  250.7 2.0 collective-permute-start.21
  253.6 2.4 collective-permute-start.9
  256.0 3.7 %collective-permute-done.9 = bf16[12,3200]{1,0:T(8,128)(2,1)S(1)} collective-permute-done((bf16[12,3200]{1,0:T(8,128)(2,1)S(1)}, bf16[12,3200]{1,0:T(8,128)(2,1)S(1)}, u32[]{:S(2)}, u32[]{:S(2)}) %collective-permute-start.9) | collective-permute-done | bytes 76832 | tf_op jit(solution)/shard_map/ppermute | solution.py:330
  260.5 3.5 %collective-permute-done.10 = bf16[6,3200]{1,0:T(8,128)(2,1)S(1)} collective-permute-done((bf16[6,3200]{1,0:T(8,128)(2,1)S(1)}, bf16[6,3200]{1,0:T(8,128)(2,1)S(1)}, u32[]{:S(2)}, u32[]{:S(2)}) %collective-permute-start.10) | collective-permute-done | bytes 38432 | tf_op jit(solution)/shard_map/ppermute | solution.py:330
  264.6 9.7 %collective-permute-done.24 = bf16[384,768]{1,0:T(8,128)(2,1)S(1)} collective-permute-done((bf16[384,768]{1,0:T(8,128)(2,1)S(1)}, bf16[384,768]{1,0:T(8,128)(2,1)S(1)}, u32[]{:S(2)}, u32[]{:S(2)}) %collective-permute-start.24) | collective-permute-done | bytes 589856 | tf_op jit(solution)/shard_map/ppermute | solution.py:330
  277.9 8.2 %collective-permute-done.25 = bf16[3,64,768]{2,0,1:T(4,128)(2,1)S(1)} collective-permute-done((bf16[3,64,768]{2,0,1:T(4,128)(2,1)S(1)}, bf16[3,64,768]{2,0,1:T(4,128)(2,1)S(1)}, u32[]{:S(2)}, u32[]{:S(2)}) %collective-permute-start.25) | collective-permute-done | bytes 294944 | tf_op jit(solution)/shard_map/ppermute | solution.py:330
  287.0 5.1 %collective-permute-done.26 = bf16[3,32,768]{2,0,1:T(4,128)(2,1)S(1)} collective-permute-done((bf16[3,32,768]{2,0,1:T(4,128)(2,1)S(1)}, bf16[3,32,768]{2,0,1:T(4,128)(2,1)S(1)}, u32[]{:S(2)}, u32[]{:S(2)}) %collective-permute-start.26) | collective-permute-done | bytes 147488 | tf_op jit(solution)/shard_map/ppermute | solution.py:330
  293.6 3.3 %collective-permute-done.27 = bf16[3,16,768]{2,0,1:T(4,128)(2,1)S(1)} collective-permute-done((bf16[3,16,768]{2,0,1:T(4,128)(2,1)S(1)}, bf16[3,16,768]{2,0,1:T(4,128)(2,1)S(1)}, u32[]{:S(2)}, u32[]{:S(2)}) %collective-permute-start.27) | collective-permute-done | bytes 73760 | tf_op jit(solution)/shard_map/ppermute | solution.py:330
  297.5 3.5 %collective-permute-start.28 = (bf16[3,8,768]{2,0,1:T(4,128)(2,1)}, bf16[3,8,768]{2,0,1:T(4,128)(2,1)}, u32[]{:S(2)}, u32[]{:S(2)}) collective-permute-start(bf16[3,8,768]{2,0,1:T(4,128)(2,1)} %fusion.38), channel_id=1, source_target_pairs={{0,1},{1,0},{2,3},{3,2},{4,5},{5,4},{6,7},{7,6},{8,9},{9,8},{10,11... | collective-permute-start | bytes 110600 | tf_op jit(solution)/shard_map/ppermute | solution.py:330
  304.3 2.2 reshape.509
  (164 shorter events, 45.4 us)
Async XLA Ops:
  7.2 92.7 %all-gather.2.cloned.1.call-start = ((), (), s32[]{:S(2)}) async-start(), calls=%async_computation | async-start | bytes 17700864 | tf_op jit(solution)/shard_map/all_gather | solution.py:391
  177.7 15.4 %copy-start.12 = (bf16[384,1536]{1,0:T(8,128)(2,1)S(1)}, bf16[384,1536]{1,0:T(8,128)(2,1)}, u32[]{:S(2)}) copy-start(bf16[384,1536]{1,0:T(8,128)(2,1)} %get-tuple-element.67) | copy-start | bytes 3538948
  177.7 15.7 %copy-start.3 = (bf16[384,1536]{1,0:T(8,128)(2,1)S(1)}, bf16[384,1536]{1,0:T(8,128)(2,1)}, u32[]{:S(2)}) copy-start(bf16[384,1536]{1,0:T(8,128)(2,1)} %get-tuple-element.69) | copy-start | bytes 3538948
  192.1 11.2 %collective-permute-start.3 = (bf16[384,128]{1,0:T(8,128)(2,1)}, bf16[384,128]{1,0:T(8,128)(2,1)S(1)}, u32[]{:S(2)}, u32[]{:S(2)}) collective-permute-start(bf16[384,128]{1,0:T(8,128)(2,1)} %get-tuple-element.72), channel_id=1, source_target_pairs={{0,16},{1,17},{2,18},{3,19},{4,20},{5,21},{6,22},{7,23},{8,24},{9,... | collective-permute-start | bytes 294920 | tf_op jit(solution)/shard_map/ppermute | solution.py:330
  192.3 6.8 %collective-permute-start.13 = (bf16[384,768]{1,0:T(8,128)(2,1)}, bf16[384,768]{1,0:T(8,128)(2,1)S(1)}, u32[]{:S(2)}, u32[]{:S(2)}) collective-permute-start(bf16[384,768]{1,0:T(8,128)(2,1)} %get-tuple-element.77), channel_id=1, source_target_pairs={{0,16},{1,17},{2,18},{3,19},{4,20},{5,21},{6,22},{7,23},{8,24},{9,... | collective-permute-start | bytes 1769480 | tf_op jit(solution)/shard_map/ppermute | solution.py:330
  192.6 7.8 %collective-permute-start.14 = (bf16[384,768]{1,0:T(8,128)(2,1)S(1)}, bf16[384,768]{1,0:T(8,128)(2,1)S(1)}, u32[]{:S(2)}, u32[]{:S(2)}) collective-permute-start(bf16[384,768]{1,0:T(8,128)(2,1)S(1)} %copy-done.14), channel_id=1, source_target_pairs={{0,16},{1,17},{2,18},{3,19},{4,20},{5,21},{6,22},{7,23},{8,24},{9,... | collective-permute-start | bytes 1769480 | tf_op jit(solution)/shard_map/ppermute | solution.py:330
  192.9 8.7 %collective-permute-start.2 = (bf16[384,1536]{1,0:T(8,128)(2,1)S(1)}, bf16[384,1536]{1,0:T(8,128)(2,1)S(1)}, u32[]{:S(2)}, u32[]{:S(2)}) collective-permute-start(bf16[384,1536]{1,0:T(8,128)(2,1)S(1)} %copy-done.13), channel_id=1, source_target_pairs={{0,16},{1,17},{2,18},{3,19},{4,20},{5,21},{6,22},{7,23},{8,24},{9,... | collective-permute-start | bytes 3538952 | tf_op jit(solution)/shard_map/ppermute | solution.py:330
  193.1 13.4 %collective-permute-start = (bf16[384,1536]{1,0:T(8,128)(2,1)S(1)}, bf16[384,1536]{1,0:T(8,128)(2,1)S(1)}, u32[]{:S(2)}, u32[]{:S(2)}) collective-permute-start(bf16[384,1536]{1,0:T(8,128)(2,1)S(1)} %copy-done.12), channel_id=1, source_target_pairs={{0,16},{1,17},{2,18},{3,19},{4,20},{5,21},{6,22},{7,23},{8,24},{9,... | collective-permute-start | bytes 3538952 | tf_op jit(solution)/shard_map/ppermute | solution.py:330
  200.1 7.2 %collective-permute-start.11 = (bf16[384,1536]{1,0:T(8,128)(2,1)S(1)}, bf16[384,1536]{1,0:T(8,128)(2,1)S(1)}, u32[]{:S(2)}, u32[]{:S(2)}) collective-permute-start(bf16[384,1536]{1,0:T(8,128)(2,1)S(1)} %copy-done.11), channel_id=1, source_target_pairs={{0,16},{1,17},{2,18},{3,19},{4,20},{5,21},{6,22},{7,23},{8,24},{9,... | collective-permute-start | bytes 3538952 | tf_op jit(solution)/shard_map/ppermute | solution.py:330
  200.9 36.8 %collective-permute-start.22 = (bf16[1536,768]{1,0:T(8,128)(2,1)S(1)}, bf16[1536,768]{1,0:T(8,128)(2,1)S(1)}, u32[]{:S(2)}, u32[]{:S(2)}) collective-permute-start(bf16[1536,768]{1,0:T(8,128)(2,1)S(1)} %copy-done.10), channel_id=1, source_target_pairs={{0,16},{1,17},{2,18},{3,19},{4,20},{5,21},{6,22},{7,23},{8,24},{9,... | collective-permute-start | bytes 7077896 | tf_op jit(solution)/shard_map/ppermute | solution.py:330
  201.6 10.0 %collective-permute-start.15 = (bf16[192,1536]{1,0:T(8,128)(2,1)S(1)}, bf16[192,1536]{1,0:T(8,128)(2,1)S(1)}, u32[]{:S(2)}, u32[]{:S(2)}) collective-permute-start(bf16[192,1536]{1,0:T(8,128)(2,1)S(1)} %get-tuple-element.109), channel_id=1, source_target_pairs={{0,3},{1,2},{2,1},{3,0},{4,7},{5,6},{6,5},{7,4},{8,11},{9,10},{10,... | collective-permute-start | bytes 1769480 | tf_op jit(solution)/shard_map/ppermute | solution.py:330
  203.7 20.6 %collective-permute-start.4 = (bf16[192,1664]{1,0:T(8,128)(2,1)S(1)}, bf16[192,1664]{1,0:T(8,128)(2,1)S(1)}, u32[]{:S(2)}, u32[]{:S(2)}) collective-permute-start(bf16[192,1664]{1,0:T(8,128)(2,1)S(1)} %get-tuple-element.103), channel_id=1, source_target_pairs={{0,12},{1,13},{2,14},{3,15},{4,8},{5,9},{6,10},{7,11},{8,4},{9,5},... | collective-permute-start | bytes 1916936 | tf_op jit(solution)/shard_map/ppermute | solution.py:330
  206.8 14.9 %collective-permute-start.1 = (bf16[192,1536]{1,0:T(8,128)(2,1)S(1)}, bf16[192,1536]{1,0:T(8,128)(2,1)S(1)}, u32[]{:S(2)}, u32[]{:S(2)}) collective-permute-start(bf16[192,1536]{1,0:T(8,128)(2,1)S(1)} %get-tuple-element.107), channel_id=1, source_target_pairs={{0,12},{1,13},{2,14},{3,15},{4,8},{5,9},{6,10},{7,11},{8,4},{9,5},... | collective-permute-start | bytes 1769480 | tf_op jit(solution)/shard_map/ppermute | solution.py:330
  207.7 14.5 %collective-permute-start.12 = (bf16[192,1536]{1,0:T(8,128)(2,1)S(1)}, bf16[192,1536]{1,0:T(8,128)(2,1)S(1)}, u32[]{:S(2)}, u32[]{:S(2)}) collective-permute-start(bf16[192,1536]{1,0:T(8,128)(2,1)S(1)} %get-tuple-element.111), channel_id=1, source_target_pairs={{0,3},{1,2},{2,1},{3,0},{4,7},{5,6},{6,5},{7,4},{8,11},{9,10},{10,... | collective-permute-start | bytes 1769480 | tf_op jit(solution)/shard_map/ppermute | solution.py:330
  211.7 17.4 %collective-permute-start.17 = (bf16[96,1536]{1,0:T(8,128)(2,1)S(1)}, bf16[96,1536]{1,0:T(8,128)(2,1)S(1)}, u32[]{:S(2)}, u32[]{:S(2)}) collective-permute-start(bf16[96,1536]{1,0:T(8,128)(2,1)S(1)} %get-tuple-element.121), channel_id=1, source_target_pairs={{0,1},{1,0},{2,3},{3,2},{4,5},{5,4},{6,7},{7,6},{8,9},{9,8},{10,11... | collective-permute-start | bytes 884744 | tf_op jit(solution)/shard_map/ppermute | solution.py:330
  221.8 9.3 %collective-permute-start.5 = (bf16[96,1536]{1,0:T(8,128)(2,1)S(1)}, bf16[96,1536]{1,0:T(8,128)(2,1)S(1)}, u32[]{:S(2)}, u32[]{:S(2)}) collective-permute-start(bf16[96,1536]{1,0:T(8,128)(2,1)S(1)} %get-tuple-element.117), channel_id=1, source_target_pairs={{0,4},{1,5},{2,6},{3,7},{4,0},{5,1},{6,2},{7,3},{8,12},{9,13},{10,... | collective-permute-start | bytes 884744 | tf_op jit(solution)/shard_map/ppermute | solution.py:330
  222.3 6.8 %collective-permute-start.16 = (bf16[96,1536]{1,0:T(8,128)(2,1)S(1)}, bf16[96,1536]{1,0:T(8,128)(2,1)S(1)}, u32[]{:S(2)}, u32[]{:S(2)}) collective-permute-start(bf16[96,1536]{1,0:T(8,128)(2,1)S(1)} %get-tuple-element.123), channel_id=1, source_target_pairs={{0,1},{1,0},{2,3},{3,2},{4,5},{5,4},{6,7},{7,6},{8,9},{9,8},{10,11... | collective-permute-start | bytes 884744 | tf_op jit(solution)/shard_map/ppermute | solution.py:330
  224.4 7.7 %collective-permute-start.6 = (bf16[96,1664]{1,0:T(8,128)(2,1)S(1)}, bf16[96,1664]{1,0:T(8,128)(2,1)S(1)}, u32[]{:S(2)}, u32[]{:S(2)}) collective-permute-start(bf16[96,1664]{1,0:T(8,128)(2,1)S(1)} %get-tuple-element.113), channel_id=1, source_target_pairs={{0,4},{1,5},{2,6},{3,7},{4,0},{5,1},{6,2},{7,3},{8,12},{9,13},{10,... | collective-permute-start | bytes 958472 | tf_op jit(solution)/shard_map/ppermute | solution.py:330
  229.3 8.0 %collective-permute-start.18 = (bf16[48,3072]{1,0:T(8,128)(2,1)S(1)}, bf16[48,3072]{1,0:T(8,128)(2,1)S(1)}, u32[]{:S(2)}, u32[]{:S(2)}) collective-permute-start(bf16[48,3072]{1,0:T(8,128)(2,1)S(1)} %get-tuple-element.119), channel_id=1, source_target_pairs={{0,96},{1,97},{2,98},{3,99},{4,100},{5,101},{6,102},{7,103},{8,104... | collective-permute-start | bytes 884744 | tf_op jit(solution)/shard_map/ppermute | solution.py:330
  232.2 15.9 %collective-permute-start.7 = (bf16[48,3200]{1,0:T(8,128)(2,1)S(1)}, bf16[48,3200]{1,0:T(8,128)(2,1)S(1)}, u32[]{:S(2)}, u32[]{:S(2)}) collective-permute-start(bf16[48,3200]{1,0:T(8,128)(2,1)S(1)} %get-tuple-element.115), channel_id=1, source_target_pairs={{0,3},{1,2},{2,1},{3,0},{4,7},{5,6},{6,5},{7,4},{8,11},{9,10},{10,... | collective-permute-start | bytes 921608 | tf_op jit(solution)/shard_map/ppermute | solution.py:330
  237.3 7.1 %collective-permute-start.19 = (bf16[24,3072]{1,0:T(8,128)(2,1)S(1)}, bf16[24,3072]{1,0:T(8,128)(2,1)S(1)}, u32[]{:S(2)}, u32[]{:S(2)}) collective-permute-start(bf16[24,3072]{1,0:T(8,128)(2,1)S(1)} %get-tuple-element.131), channel_id=1, source_target_pairs={{0,32},{1,33},{2,34},{3,35},{4,36},{5,37},{6,38},{7,39},{8,40},{9,... | collective-permute-start | bytes 442376 | tf_op jit(solution)/shard_map/ppermute | solution.py:330
  238.4 25.6 %collective-permute-start.23 = (bf16[768,768]{1,0:T(8,128)(2,1)S(1)}, bf16[768,768]{1,0:T(8,128)(2,1)S(1)}, u32[]{:S(2)}, u32[]{:S(2)}) collective-permute-start(bf16[768,768]{1,0:T(8,128)(2,1)S(1)} %get-tuple-element.101), channel_id=1, source_target_pairs={{0,96},{1,97},{2,98},{3,99},{4,100},{5,101},{6,102},{7,103},{8,104... | collective-permute-start | bytes 3538952 | tf_op jit(solution)/shard_map/ppermute | solution.py:330
  244.5 6.2 %collective-permute-start.20 = (bf16[12,3072]{1,0:T(8,128)(2,1)S(1)}, bf16[12,3072]{1,0:T(8,128)(2,1)S(1)}, u32[]{:S(2)}, u32[]{:S(2)}) collective-permute-start(bf16[12,3072]{1,0:T(8,128)(2,1)S(1)} %get-tuple-element.139), channel_id=1, source_target_pairs={{0,12},{1,13},{2,14},{3,15},{4,8},{5,9},{6,10},{7,11},{8,4},{9,5},... | collective-permute-start | bytes 221192 | tf_op jit(solution)/shard_map/ppermute | solution.py:330
  248.2 5.4 %collective-permute-start.8 = (bf16[24,3200]{1,0:T(8,128)(2,1)S(1)}, bf16[24,3200]{1,0:T(8,128)(2,1)S(1)}, u32[]{:S(2)}, u32[]{:S(2)}) collective-permute-start(bf16[24,3200]{1,0:T(8,128)(2,1)S(1)} %get-tuple-element.129), channel_id=1, source_target_pairs={{0,1},{1,0},{2,3},{3,2},{4,5},{5,4},{6,7},{7,6},{8,9},{9,8},{10,11... | collective-permute-start | bytes 460808 | tf_op jit(solution)/shard_map/ppermute | solution.py:330
  250.7 5.3 %collective-permute-start.21 = (bf16[6,3072]{1,0:T(8,128)(2,1)S(1)}, bf16[6,3072]{1,0:T(8,128)(2,1)S(1)}, u32[]{:S(2)}, u32[]{:S(2)}) collective-permute-start(bf16[6,3072]{1,0:T(8,128)(2,1)S(1)} %fusion.41), channel_id=1, source_target_pairs={{0,4},{1,5},{2,6},{3,7},{4,0},{5,1},{6,2},{7,3},{8,12},{9,13},{10,... | collective-permute-start | bytes 110600 | tf_op jit(solution)/shard_map/ppermute | solution.py:330
  253.6 6.1 %collective-permute-start.9 = (bf16[12,3200]{1,0:T(8,128)(2,1)S(1)}, bf16[12,3200]{1,0:T(8,128)(2,1)S(1)}, u32[]{:S(2)}, u32[]{:S(2)}) collective-permute-start(bf16[12,3200]{1,0:T(8,128)(2,1)S(1)} %get-tuple-element.137), channel_id=1, source_target_pairs={{0,96},{1,97},{2,98},{3,99},{4,100},{5,101},{6,102},{7,103},{8,104... | collective-permute-start | bytes 230408 | tf_op jit(solution)/shard_map/ppermute | solution.py:330
  259.8 4.2 %collective-permute-start.10 = (bf16[6,3200]{1,0:T(8,128)(2,1)S(1)}, bf16[6,3200]{1,0:T(8,128)(2,1)S(1)}, u32[]{:S(2)}, u32[]{:S(2)}) collective-permute-start(bf16[6,3200]{1,0:T(8,128)(2,1)S(1)} %fusion.34), channel_id=1, source_target_pairs={{0,32},{1,33},{2,34},{3,35},{4,36},{5,37},{6,38},{7,39},{8,40},{9,... | collective-permute-start | bytes 115208 | tf_op jit(solution)/shard_map/ppermute | solution.py:330
  264.4 10.0 %collective-permute-start.24 = (bf16[384,768]{1,0:T(8,128)(2,1)S(1)}, bf16[384,768]{1,0:T(8,128)(2,1)S(1)}, u32[]{:S(2)}, u32[]{:S(2)}) collective-permute-start(bf16[384,768]{1,0:T(8,128)(2,1)S(1)} %get-tuple-element.105), channel_id=1, source_target_pairs={{0,32},{1,33},{2,34},{3,35},{4,36},{5,37},{6,38},{7,39},{8,40},{9,... | collective-permute-start | bytes 1769480 | tf_op jit(solution)/shard_map/ppermute | solution.py:330
  274.9 11.2 %collective-permute-start.25 = (bf16[3,64,768]{2,0,1:T(4,128)(2,1)S(1)}, bf16[3,64,768]{2,0,1:T(4,128)(2,1)S(1)}, u32[]{:S(2)}, u32[]{:S(2)}) collective-permute-start(bf16[3,64,768]{2,0,1:T(4,128)(2,1)S(1)} %fusion.10), channel_id=1, source_target_pairs={{0,12},{1,13},{2,14},{3,15},{4,8},{5,9},{6,10},{7,11},{8,4},{9,5},... | collective-permute-start | bytes 884744 | tf_op jit(solution)/shard_map/ppermute | solution.py:330
  286.3 5.7 %collective-permute-start.26 = (bf16[3,32,768]{2,0,1:T(4,128)(2,1)S(1)}, bf16[3,32,768]{2,0,1:T(4,128)(2,1)S(1)}, u32[]{:S(2)}, u32[]{:S(2)}) collective-permute-start(bf16[3,32,768]{2,0,1:T(4,128)(2,1)S(1)} %get-tuple-element.125), channel_id=1, source_target_pairs={{0,4},{1,5},{2,6},{3,7},{4,0},{5,1},{6,2},{7,3},{8,12},{9,13},{10,... | collective-permute-start | bytes 442376 | tf_op jit(solution)/shard_map/ppermute | solution.py:330
  292.2 4.7 %collective-permute-start.27 = (bf16[3,16,768]{2,0,1:T(4,128)(2,1)S(1)}, bf16[3,16,768]{2,0,1:T(4,128)(2,1)S(1)}, u32[]{:S(2)}, u32[]{:S(2)}) collective-permute-start(bf16[3,16,768]{2,0,1:T(4,128)(2,1)S(1)} %get-tuple-element.133), channel_id=1, source_target_pairs={{0,3},{1,2},{2,1},{3,0},{4,7},{5,6},{6,5},{7,4},{8,11},{9,10},{10,... | collective-permute-start | bytes 221192 | tf_op jit(solution)/shard_map/ppermute | solution.py:330
  297.5 8.9 %collective-permute-start.28 = (bf16[3,8,768]{2,0,1:T(4,128)(2,1)}, bf16[3,8,768]{2,0,1:T(4,128)(2,1)}, u32[]{:S(2)}, u32[]{:S(2)}) collective-permute-start(bf16[3,8,768]{2,0,1:T(4,128)(2,1)} %fusion.38), channel_id=1, source_target_pairs={{0,1},{1,0},{2,3},{3,2},{4,5},{5,4},{6,7},{7,6},{8,9},{9,8},{10,11... | collective-permute-start | bytes 110600 | tf_op jit(solution)/shard_map/ppermute | solution.py:330
  (13 other events, 54.6 us)
Sparse Core Ops, SparseCore 0:
  16.8 83.1 all-gather.1
